TPU v7x, 512 devices: a whole 4x4x16 slice. The times are simulated.
512 devices in a mesh: frame: 64 (over z, x_lo, core), row: 8 (over y, x_hi).
Axes of the slice: x: 4 (x_hi: 2, x_lo: 2; x = x_hi * 2 + x_lo), y: 4, z: 16, core: 2. Of those that a mesh axis runs over, the one named last changes fastest.
Arguments:
- video: bfloat16 [64, 32, 32, 3072], P('frame', 'row'), may hold values from -18 to 18
- qkv_weight: bfloat16 [3072, 3, 2048], P('frame', None, 'row'), may hold values from -1 to 1
- window: int32 [16, 3], P('row'), may hold values from 0 to 1, as said below
- clips: int32 [64], replicated, may hold values from 0 to 15, never falling along the last dimension, each value on 1 to 8 neighbouring positions
Outputs:
- attended: bfloat16 [64, 32, 32, 2048], P('frame', None, None, 'row')
Inputs may be any that keep to these rules, and one draw needn't show every extreme that they name: window[h, 0], window[h, 1] and window[h, 2] are head h's reaches along frames, row tiles and column tiles; in every group of 2 consecutive heads along each of the three, some head has reach 1. `clips`: clip numbers never fall along the frames; each clip has 1 to 8 frames.
All inputs are finite; a program needn't handle non-finite values.
Results may differ from a plain program's by a relative error of at most 0.0068.
Values may be sent and summed in bfloat16 or wider, within the bound.
No kernel may reach another device: no remote copies, remote signals or barrier semaphores. Data moves between devices by JAX's collectives and lax.ppermute only.
A program may use at most 64 MiB of HBM per device.

v0:
```python
import math
import jax
import jax.numpy as jnp
from jax import lax
from jax.sharding import PartitionSpec as P

HD = 128
TH = 8
TW = 8


def with_halo(value, sides, width):
    for axis, dim in sides:
        count, length = (lax.axis_size(axis), value.shape[dim])
        up = [(i, (i + 1) % count) for i in range(count - 1)]
        down = [(j, i) for i, j in up]
        last = lax.slice_in_dim(value, length - width, length, axis=dim)
        initial = lax.slice_in_dim(value, 0, width, axis=dim)
        before = lax.ppermute(last, axis, up)
        after = lax.ppermute(initial, axis, down)
        value = jnp.concatenate([before, value, after], axis=dim)
    return value


def body(video, qkv_weight, window, clips):
    frame_here = lax.axis_index("frame")
    local_width = qkv_weight.shape[2]
    head_count = local_width // HD
    features = video.shape[3]
    qkv_matrix = lax.all_gather(qkv_weight, "frame", axis=0, tiled=True).reshape(
        features, 3 * local_width
    )
    shard_rows = lax.all_gather(video, "row", axis=1, tiled=True)
    flattened = shard_rows.reshape(-1, features)
    result = jnp.dot(flattened, qkv_matrix, preferred_element_type=jnp.float32).astype(jnp.bfloat16)
    projected = result.reshape(
        shard_rows.shape[0], shard_rows.shape[1], shard_rows.shape[2], 3 * local_width
    )
    row_count = projected.shape[1]
    col_count = projected.shape[2]
    tokens = row_count * col_count
    projected = projected.reshape(tokens, 3 * local_width)
    queries = projected[:, :local_width]
    keyval = projected[:, local_width:].reshape(1, tokens, 2 * local_width)
    nearby = with_halo(keyval, (("frame", 0),), 1)
    edge_clip = jnp.full((1,), -1, jnp.int32)
    padded_clips = jnp.concatenate([edge_clip, clips, edge_clip])
    nearby_clips = lax.dynamic_slice_in_dim(padded_clips, frame_here, 3, 0)
    same_clip = nearby_clips == nearby_clips[1]
    frame_gap = jnp.abs(jnp.arange(3) - 1)
    frame_allowed = (frame_gap[None, :] <= window[:, 0:1]) & same_clip[None, :]
    tile_count = row_count // TH
    block_tiles = tile_count
    while block_tiles % 2 == 0 and block_tiles * TH * col_count > 512:
        block_tiles = block_tiles // 2
    band_tiles = min(tile_count, block_tiles + 2)
    positions = jnp.arange(tokens)
    tile_row = positions // col_count // TH
    tile_column = positions % col_count // TW
    score_scale = 1.0 / math.sqrt(HD)
    outputs = []
    for block_index in range(tile_count // block_tiles):
        first_tile = block_index * block_tiles
        band_start = min(max(first_tile - 1, 0), tile_count - band_tiles)
        query_from = first_tile * TH * col_count
        query_count = block_tiles * TH * col_count
        key_from = band_start * TH * col_count
        key_count = band_tiles * TH * col_count
        row_gap = jnp.abs(
            tile_row[query_from : query_from + query_count, None]
            - tile_row[None, key_from : key_from + key_count]
        )
        column_gap = jnp.abs(
            tile_column[query_from : query_from + query_count, None]
            - tile_column[None, key_from : key_from + key_count]
        )
        head_blocks = []
        for head_index in range(head_count):
            low = head_index * HD
            query_head = queries[query_from : query_from + query_count, low : low + HD]
            key_head = nearby[:, :, low : low + HD].reshape(3 * key_count, HD)
            value_head = nearby[:, :, local_width + low : local_width + low + HD].reshape(
                3 * key_count, HD
            )
            scores = (
                lax.dot_general(
                    query_head,
                    key_head,
                    (((1,), (1,)), ((), ())),
                    preferred_element_type=jnp.float32,
                )
                * score_scale
            )
            inside = (row_gap <= window[head_index, 1]) & (column_gap <= window[head_index, 2])
            allowed = (frame_allowed[head_index][None, :, None] & inside[:, None, :]).reshape(
                query_count, 3 * key_count
            )
            masked = jnp.where(allowed, scores, -1e30)
            row_max = jnp.max(masked, axis=1, keepdims=True)
            weight = jnp.exp(masked - row_max)
            totals = jnp.sum(weight, axis=1, keepdims=True)
            blended = (
                jnp.dot(weight.astype(jnp.bfloat16), value_head, preferred_element_type=jnp.float32)
                / totals
            )
            head_blocks.append(blended.astype(jnp.bfloat16))
        outputs.append(jnp.concatenate(head_blocks, axis=1))
    attended = jnp.concatenate(outputs, axis=0)
    return attended.reshape(1, row_count, col_count, local_width)


def solution(mesh):
    placed = (P("frame", "row", None, None), P("frame", None, "row"), P("row", None), P())
    return jax.shard_map(
        body, mesh=mesh, in_specs=placed, out_specs=P("frame", None, None, "row"), check_vma=False
    )
```

profile of v0, /device:TPU:98, one launch (start us, length us, event | category | flops | bytes accessed | tf_op | source)
XLA Modules:
  0.0 308.2 jit_solution(17706026127067027402)
XLA Ops:
  6.5 0.0 all-gather.5.cloned.1.call-start
  6.5 0.7 all-gather.5.cloned.1.call-update
  7.3 0.0 all-gather.3.cloned.1.call-start
  7.3 0.7 all-gather.3.cloned.1.call-update
  8.0 1.5 fusion.80
  9.5 128.0 %all-gather.5.cloned.1.call-done = bf16[3072,3,256]{2,0,1:T(8,128)(2,1)} async-done(((bf16[48,3,256]{2,0,1:T(8,128)(2,1)}), bf16[3072,3,256]{2,0,1:T(8,128)(2,1)}) %all-gather.5.cloned.1.call-update) | async-done | bytes 4718608 | tf_op jit(solution)/shard_map/all_gather | solution.py:30
  137.5 6.7 %copy.14 = bf16[3072,3,256]{0,2,1:T(8,128)(2,1)} copy(bf16[3072,3,256]{2,0,1:T(8,128)(2,1)} %all-gather.5.cloned.1.call-done) | data formatting | bytes 9437184 | tf_op jit(solution)/shard_map/all_gather | solution.py:30
  144.1 97.2 %all-gather.3.cloned.1.call-done = bf16[1,32,32,3072]{3,2,0,1:T(8,128)(2,1)} async-done(((bf16[1,4,32,3072]{3,2,0,1:T(8,128)(2,1)}), bf16[1,32,32,3072]{3,2,0,1:T(8,128)(2,1)}) %all-gather.3.cloned.1.call-update) | async-done | bytes 6291472 | tf_op jit(solution)/shard_map/all_gather | solution.py:33
  241.3 8.6 %convolution_convert_fusion = bf16[1024,768]{1,0:T(8,128)(2,1)S(1)} fusion(bf16[1024,3072]{1,0:T(8,128)(2,1)} %bitcast.47, bf16[3072,768]{0,1:T(8,128)(2,1)} %bitcast.45), kind=kOutput, calls=%fused_computation.41 | convolution fusion | flops 4832624640 | bytes 12582912 | tf_op jit(solution)/shard_map/dot_general | solution.py:35
  249.9 0.0 copy-start
  249.9 1.1 slice_bitcast_fusion
  251.0 2.4 collective-permute-start.1
  253.4 1.9 collective-permute-start
  255.4 6.5 %fusion.28 = (pred[512,1024]{0,1:T(8,128)(4,1)}, pred[512,1024]{0,1:T(8,128)(4,1)}, pred[512,1024]{0,1:T(8,128)(4,1)S(1)}, pred[512,1024]{0,1:T(8,128)(4,1)S(1)}) fusion(s32[]{:T(128)} %bitcast.3, s32[1024]{0:T(1024)S(1)} %get-tuple-element.33, s32[512]{0:T(512)S(1)} %get-tuple-element.17, s32[]{:T(128)} %bitcast.2, s32[1024]{0:T(1024)S(1)} %get-tuple-element.34, ...), kind=kLoop, calls=%fused_computation.37 | loop fusion | flops 10485760 | bytes 2113552 | tf_op jit(solution)/shard_map/and | solution.py:94
  261.9 0.0 copy-start.4
  261.9 0.0 copy-start.3
  261.9 0.4 and.210
  262.3 0.0 copy-done
  262.3 1.7 copy.17
  264.0 0.0 copy-done.4
  264.0 0.1 pad_add_fusion
  264.1 0.1 dynamic_slice.3
  264.2 0.6 slice.87
  264.8 0.7 broadcast_compare_fusion
  265.5 0.0 copy-done.3
  265.5 0.1 slice_reduce_fusion
  265.6 0.1 compare_and_fusion
  265.7 0.1 and.198
  265.8 0.4 and.206
  266.2 1.7 copy.16
  267.9 0.1 and.186
  268.0 0.0 copy-start.2
  268.0 1.5 and.202
  269.6 1.7 copy.15
  271.3 0.0 copy-done.2
  271.3 0.4 and.194
  271.7 1.7 copy.12
  273.4 3.9 %collective-permute-done.1 = bf16[1,1024,512]{2,1,0:T(8,128)(2,1)} collective-permute-done((bf16[1,1024,512]{2,1,0:T(8,128)(2,1)}, bf16[1,1024,512]{2,1,0:T(8,128)(2,1)}, u32[]{:S(2)}, u32[]{:S(2)}) %collective-permute-start.1) | collective-permute-done | bytes 1048608 | tf_op jit(solution)/shard_map/ppermute | solution.py:20
  277.3 3.6 %collective-permute-done = bf16[1,1024,512]{2,1,0:T(8,128)(2,1)} collective-permute-done((bf16[1,1024,512]{2,1,0:T(8,128)(2,1)}, bf16[1,1024,512]{2,1,0:T(8,128)(2,1)}, u32[]{:S(2)}, u32[]{:S(2)}) %collective-permute-start) | collective-permute-done | bytes 1048608 | tf_op jit(solution)/shard_map/ppermute | solution.py:19
  280.9 2.2 pad_maximum_fusion
  283.1 0.0 copy-start.1
  283.1 0.6 fusion.77
  283.7 0.8 copy-done.1
  284.5 1.6 fusion.81
  286.2 1.9 fusion.83
  288.0 1.0 fusion.6
  289.0 1.3 fusion.53
  290.3 1.0 fusion.2
  291.3 1.3 fusion.41
  292.6 1.6 fusion.82
  294.2 1.6 fusion.84
  295.8 1.0 fusion.4
  296.8 1.3 fusion.47
  298.1 1.0 fusion
  299.1 1.3 fusion.35
  300.3 0.1 maximum_maximum_fusion
  300.4 1.0 copy.18
  (7 shorter events, 0.1 us)
Async XLA Ops:
  6.5 130.9 %all-gather.5.cloned.1.call-start = ((), (), s32[]{:S(2)}) async-start(), calls=%async_computation.1 | async-start | bytes 4792320 | tf_op jit(solution)/shard_map/all_gather | solution.py:30
  7.3 234.1 %all-gather.3.cloned.1.call-start = ((), (), s32[]{:S(2)}) async-start(), calls=%async_computation | async-start | bytes 7077888 | tf_op jit(solution)/shard_map/all_gather | solution.py:33
  249.9 12.4 %copy-start = (bf16[1024,768]{1,0:T(8,128)(2,1)}, bf16[1024,768]{1,0:T(8,128)(2,1)S(1)}, u32[]{:S(2)}) copy-start(bf16[1024,768]{1,0:T(8,128)(2,1)S(1)} %convolution_convert_fusion) | copy-start | bytes 4718596
  251.0 26.2 %collective-permute-start.1 = (bf16[1,1024,512]{2,1,0:T(8,128)(2,1)}, bf16[1,1024,512]{2,1,0:T(8,128)(2,1)}, u32[]{:S(2)}, u32[]{:S(2)}) collective-permute-start(bf16[1,1024,512]{2,1,0:T(8,128)(2,1)} %slice_bitcast_fusion), channel_id=1, source_target_pairs={{8,0},{16,8},{24,16},{32,24},{40,32},{48,40},{56,48},{64,56},{72,6... | collective-permute-start | bytes 3145736 | tf_op jit(solution)/shard_map/ppermute | solution.py:20
  253.4 27.5 %collective-permute-start = (bf16[1,1024,512]{2,1,0:T(8,128)(2,1)}, bf16[1,1024,512]{2,1,0:T(8,128)(2,1)}, u32[]{:S(2)}, u32[]{:S(2)}) collective-permute-start(bf16[1,1024,512]{2,1,0:T(8,128)(2,1)} %slice_bitcast_fusion), channel_id=1, source_target_pairs={{0,8},{8,16},{16,24},{24,32},{32,40},{40,48},{48,56},{56,64},{64,7... | collective-permute-start | bytes 3145736 | tf_op jit(solution)/shard_map/ppermute | solution.py:19
  261.9 2.1 copy-start.4
  261.9 3.6 %copy-start.3 = (s32[2,3]{1,0:T(2,128)S(1)}, s32[2,3]{1,0:T(2,128)}, u32[]{:S(2)}) copy-start(s32[2,3]{1,0:T(2,128)} %param.6) | copy-start | bytes 76
  268.0 3.2 %copy-start.2 = (pred[512,1024]{0,1:T(8,128)(4,1)S(1)}, pred[512,1024]{0,1:T(8,128)(4,1)}, u32[]{:S(2)}) copy-start(pred[512,1024]{0,1:T(8,128)(4,1)} %get-tuple-element.9) | copy-start | bytes 1572868
  283.1 1.4 copy-start.1
Sparse Core Ops, SparseCore 0:
  9.5 127.9 all-gather.4
  140.6 100.6 all-gather.2
where the time goes:
time: 309 us; the launch traced here: 308 us
  waiting for transfers between devices  234 us (76%)
  local copies, waits for them, and re-layouts  22.2 us (7%)
  matrix products  20.4 us (7%)
  other arithmetic  13.6 us (4%)
  between operations  13.6 us (4%)
  starting transfers between devices  4.36 us (1%)
    all_gather x1, waiting for transfers between devices, body(): lax.all_gather(qkv_weight, 'frame', axis=0, tiled=True)  128 us
    all_gather x1, waiting for transfers between devices, body(): shard_rows = lax.all_gather(video, 'row', axis=1, tiled=True)  97.2 us
    and x13, local copies, waits for them, and re-layouts, body(): frame_allowed[head_index][None, :, None] & inside[:, None, :]  9.75 us
    dot_general x1, matrix products, body(): jnp.dot(flattened, qkv_matrix, preferred_element_type=jnp.float32)  8.6 us
    dot_general x4, matrix products, body(): lax.dot_general(query_head, key_head, (((1,), (1,)), ((), ())), preferred...  6.75 us
    all_gather x1, local copies, waits for them, and re-layouts, body(): lax.all_gather(qkv_weight, 'frame', axis=0, tiled=True)  6.67 us
    and x1, other arithmetic, body(): (row_gap <= window[head_index, 1]) & (column_gap <= window[head_index, 2])  6.53 us
  transfers between devices with their start and end apart: 4, of which 4 were waited for; matrix products, arithmetic and copies ran while one was open for 8% of the time, Pallas kernels for 0%

commit v1 on v0

--- a/solution.py
+++ b/solution.py
@@ -30,7 +30,9 @@
     qkv_matrix = lax.all_gather(qkv_weight, "frame", axis=0, tiled=True).reshape(
         features, 3 * local_width
     )
-    shard_rows = lax.all_gather(video, "row", axis=1, tiled=True)
+    shard_rows = jnp.concatenate(
+        lax.all_to_all(jnp.stack([video] * lax.axis_size("row")), "row", 0, 0), axis=1
+    )
     flattened = shard_rows.reshape(-1, features)
     result = jnp.dot(flattened, qkv_matrix, preferred_element_type=jnp.float32).astype(jnp.bfloat16)
     projected = result.reshape(

time: 309 us -> 212 us (0.69)
  the two profiles are of different devices: /device:TPU:98 before, /device:TPU:6 now
where the time goes in v1:
time: 212 us
  waiting for transfers between devices  126 us (59%)
  local copies, waits for them, and re-layouts  26 us (12%)
  matrix products  20.4 us (10%)
  other arithmetic  13.7 us (6%)
  between operations  13.6 us (6%)
  starting transfers between devices  12 us (6%)
    all_gather x1, waiting for transfers between devices, body(): lax.all_gather(qkv_weight, 'frame', axis=0, tiled=True)  119 us
    and x13, local copies, waits for them, and re-layouts, body(): frame_allowed[head_index][None, :, None] & inside[:, None, :]  9.75 us
    dot_general x1, matrix products, body(): jnp.dot(flattened, qkv_matrix, preferred_element_type=jnp.float32)  8.6 us
    all_to_all x1, starting transfers between devices, body(): lax.all_to_all(jnp.stack([video] * lax.axis_size('row')), 'row', 0, 0)  7.56 us
    dot_general x4, matrix products, body(): lax.dot_general(query_head, key_head, (((1,), (1,)), ((), ())), preferred...  6.75 us
    all_gather x1, local copies, waits for them, and re-layouts, body(): lax.all_gather(qkv_weight, 'frame', axis=0, tiled=True)  6.66 us
    and x1, other arithmetic, body(): (row_gap <= window[head_index, 1]) & (column_gap <= window[head_index, 2])  6.58 us
    ppermute x1, waiting for transfers between devices, with_halo(): before = lax.ppermute(last, axis, up)  6.4 us
  transfers between devices with their start and end apart: 4, of which 2 were waited for; matrix products, arithmetic and copies ran while one was open for 14% of the time, Pallas kernels for 0%

profile of v1, /device:TPU:6, one launch (start us, length us, event | category | flops | bytes accessed | tf_op | source)
XLA Modules:
  0.0 211.9 jit_solution(4767446225378603112)
XLA Ops:
  6.5 0.0 all-gather.2.cloned.1.call-start
  6.5 0.7 all-gather.2.cloned.1.call-update
  7.3 4.6 %stack.2 = bf16[8,1,4,32,3072]{4,3,2,1,0:T(8,128)(2,1)} broadcast(bf16[4,32,3072]{2,1,0:T(8,128)(2,1)} %bitcast.46), dimensions={2,3,4} | broadcast | bytes 7077888 | tf_op jit(solution)/shard_map/stack | solution.py:34
  11.8 0.0 copy-start.3
  11.8 7.6 %all-to-all-start = ((bf16[8,1,4,32,3072]{4,3,2,1,0:T(8,128)(2,1)}), bf16[8,1,4,32,3072]{4,3,2,1,0:T(8,128)(2,1)}, u32[]{:S(2)}, u32[]{:S(2)}) async-start(bf16[8,1,4,32,3072]{4,3,2,1,0:T(8,128)(2,1)} %stack.2), calls=%async_computation | async-start | bytes 12582912 | tf_op jit(solution)/shard_map/all_to_all | solution.py:34
  19.4 0.0 copy-done.3
  19.4 0.7 fusion.80
  20.1 119.0 %all-gather.2.cloned.1.call-done = bf16[3072,3,256]{2,0,1:T(8,128)(2,1)} async-done(((bf16[48,3,256]{2,0,1:T(8,128)(2,1)}), bf16[3072,3,256]{2,0,1:T(8,128)(2,1)}) %all-gather.2.cloned.1.call-update) | async-done | bytes 4718608 | tf_op jit(solution)/shard_map/all_gather | solution.py:30
  139.2 6.7 %copy.13 = bf16[3072,3,256]{0,2,1:T(8,128)(2,1)} copy(bf16[3072,3,256]{2,0,1:T(8,128)(2,1)} %all-gather.2.cloned.1.call-done) | data formatting | bytes 9437184 | tf_op jit(solution)/shard_map/all_gather | solution.py:30
  145.8 0.0 all-to-all-done
  145.8 8.6 %convolution_convert_fusion = bf16[1024,768]{1,0:T(8,128)(2,1)S(1)} fusion(bf16[1024,3072]{1,0:T(8,128)(2,1)} %bitcast.6, bf16[3072,768]{0,1:T(8,128)(2,1)} %bitcast.45), kind=kOutput, calls=%fused_computation.41 | convolution fusion | flops 4832624640 | bytes 12582912 | tf_op jit(solution)/shard_map/dot_general | solution.py:37
  154.4 0.0 copy-start
  154.4 1.1 slice_bitcast_fusion
  155.6 2.5 %collective-permute-start.1 = (bf16[1,1024,512]{2,1,0:T(8,128)(2,1)}, bf16[1,1024,512]{2,1,0:T(8,128)(2,1)}, u32[]{:S(2)}, u32[]{:S(2)}) collective-permute-start(bf16[1,1024,512]{2,1,0:T(8,128)(2,1)} %slice_bitcast_fusion), channel_id=1, source_target_pairs={{8,0},{16,8},{24,16},{32,24},{40,32},{48,40},{56,48},{64,56},{72,6... | collective-permute-start | bytes 3145736 | tf_op jit(solution)/shard_map/ppermute | solution.py:20
  158.1 1.9 collective-permute-start
  160.0 6.6 %fusion.28 = (pred[512,1024]{0,1:T(8,128)(4,1)}, pred[512,1024]{0,1:T(8,128)(4,1)}, pred[512,1024]{0,1:T(8,128)(4,1)S(1)}, pred[512,1024]{0,1:T(8,128)(4,1)S(1)}) fusion(s32[]{:T(128)} %bitcast.3, s32[1024]{0:T(1024)S(1)} %get-tuple-element.33, s32[512]{0:T(512)S(1)} %get-tuple-element.17, s32[]{:T(128)} %bitcast.2, s32[1024]{0:T(1024)S(1)} %get-tuple-element.34, ...), kind=kLoop, calls=%fused_computation.37 | loop fusion | flops 10485760 | bytes 2113552 | tf_op jit(solution)/shard_map/and | solution.py:96
  166.6 0.0 copy-start.4
  166.6 0.4 and.210
  167.0 0.0 copy-done
  167.0 1.7 copy.16
  168.7 0.0 copy-done.4
  168.7 0.1 pad_add_fusion
  168.8 0.1 dynamic_slice.3
  168.9 0.6 slice.87
  169.5 0.7 broadcast_compare_fusion
  170.2 0.1 slice_reduce_fusion
  170.3 0.1 compare_and_fusion
  170.4 0.1 and.198
  170.5 0.4 and.206
  170.9 1.7 copy.15
  172.6 0.1 and.186
  172.7 0.0 copy-start.2
  172.7 1.5 and.202
  174.2 1.7 copy.14
  175.9 0.0 copy-done.2
  176.0 0.4 and.194
  176.4 1.7 copy.12
  178.1 0.0 collective-permute-done.1
  178.1 6.4 %collective-permute-done = bf16[1,1024,512]{2,1,0:T(8,128)(2,1)} collective-permute-done((bf16[1,1024,512]{2,1,0:T(8,128)(2,1)}, bf16[1,1024,512]{2,1,0:T(8,128)(2,1)}, u32[]{:S(2)}, u32[]{:S(2)}) %collective-permute-start) | collective-permute-done | bytes 1048608 | tf_op jit(solution)/shard_map/ppermute | solution.py:19
  184.5 2.2 %pad_maximum_fusion = bf16[3,1024,512]{2,1,0:T(8,128)(2,1)S(1)} fusion(bf16[1,1024,512]{2,1,0:T(8,128)(2,1)} %collective-permute-done.1, bf16[1,1024,512]{2,1,0:T(8,128)(2,1)} %slice_bitcast_fusion, bf16[1,1024,512]{2,1,0:T(8,128)(2,1)} %collective-permute-done), kind=kLoop, calls=%fused_computation.20 | loop fusion | flops 3145728 | bytes 6291456 | tf_op jit(solution)/shard_map/concatenate | solution.py:21
  186.7 0.0 copy-start.1
  186.7 0.6 fusion.77
  187.3 0.8 copy-done.1
  188.1 1.6 fusion.81
  189.8 1.9 fusion.83
  191.6 1.0 fusion.6
  192.6 1.3 fusion.53
  193.9 1.0 fusion.2
  194.9 1.3 fusion.41
  196.2 1.6 fusion.82
  197.8 1.6 fusion.84
  199.4 1.0 fusion.4
  200.4 1.3 fusion.47
  201.7 1.0 fusion
  202.7 1.3 fusion.35
  204.0 0.1 maximum_maximum_fusion
  204.0 1.0 copy.17
  (7 shorter events, 0.1 us)
Async XLA Ops:
  6.5 132.6 %all-gather.2.cloned.1.call-start = ((), (), s32[]{:S(2)}) async-start(), calls=%async_computation.1 | async-start | bytes 4792320 | tf_op jit(solution)/shard_map/all_gather | solution.py:30
  11.8 7.6 %copy-start.3 = (s32[2,3]{1,0:T(2,128)S(1)}, s32[2,3]{1,0:T(2,128)}, u32[]{:S(2)}) copy-start(s32[2,3]{1,0:T(2,128)} %param.6) | copy-start | bytes 76
  11.8 134.0 %all-to-all-start = ((bf16[8,1,4,32,3072]{4,3,2,1,0:T(8,128)(2,1)}), bf16[8,1,4,32,3072]{4,3,2,1,0:T(8,128)(2,1)}, u32[]{:S(2)}, u32[]{:S(2)}) async-start(bf16[8,1,4,32,3072]{4,3,2,1,0:T(8,128)(2,1)} %stack.2), calls=%async_computation | async-start | bytes 12582912 | tf_op jit(solution)/shard_map/all_to_all | solution.py:34
  154.4 12.6 %copy-start = (bf16[1024,768]{1,0:T(8,128)(2,1)}, bf16[1024,768]{1,0:T(8,128)(2,1)S(1)}, u32[]{:S(2)}) copy-start(bf16[1024,768]{1,0:T(8,128)(2,1)S(1)} %convolution_convert_fusion) | copy-start | bytes 4718596
  155.6 22.6 %collective-permute-start.1 = (bf16[1,1024,512]{2,1,0:T(8,128)(2,1)}, bf16[1,1024,512]{2,1,0:T(8,128)(2,1)}, u32[]{:S(2)}, u32[]{:S(2)}) collective-permute-start(bf16[1,1024,512]{2,1,0:T(8,128)(2,1)} %slice_bitcast_fusion), channel_id=1, source_target_pairs={{8,0},{16,8},{24,16},{32,24},{40,32},{48,40},{56,48},{64,56},{72,6... | collective-permute-start | bytes 3145736 | tf_op jit(solution)/shard_map/ppermute | solution.py:20
  158.1 26.4 %collective-permute-start = (bf16[1,1024,512]{2,1,0:T(8,128)(2,1)}, bf16[1,1024,512]{2,1,0:T(8,128)(2,1)}, u32[]{:S(2)}, u32[]{:S(2)}) collective-permute-start(bf16[1,1024,512]{2,1,0:T(8,128)(2,1)} %slice_bitcast_fusion), channel_id=1, source_target_pairs={{0,8},{8,16},{16,24},{24,32},{32,40},{40,48},{48,56},{56,64},{64,7... | collective-permute-start | bytes 3145736 | tf_op jit(solution)/shard_map/ppermute | solution.py:19
  166.6 2.1 %copy-start.4 = (s32[64]{0:T(128)S(1)}, s32[64]{0:T(128)}, u32[]{:S(2)}) copy-start(s32[64]{0:T(128)} %param.7) | copy-start | bytes 772
  172.7 3.2 %copy-start.2 = (pred[512,1024]{0,1:T(8,128)(4,1)S(1)}, pred[512,1024]{0,1:T(8,128)(4,1)}, u32[]{:S(2)}) copy-start(pred[512,1024]{0,1:T(8,128)(4,1)} %get-tuple-element.9) | copy-start | bytes 1572868
  186.7 1.4 copy-start.1
Sparse Core Ops, SparseCore 0:
  9.5 129.6 all-gather.1
